TPU v7x, 512 devices: a whole 4x8x8 slice. The times are simulated.
512 devices in a mesh: dom: 128 (over x, y_lo, z), sub: 4 (over y_hi, core).
Axes of the slice: x: 4, y: 8 (y_hi: 2, y_lo: 4; y = y_hi * 4 + y_lo), z: 8, core: 2. Of those that a mesh axis runs over, the one named last changes fastest.
Arguments:
- left_emb: float32 [262144, 256], P(('dom', 'sub')), may hold values from -1.5 to 1.5
- left_state: float32 [262144], P(('dom', 'sub')), may hold values from 0.003 to 0.3
- right_emb: float32 [131072, 256], P(('dom', 'sub')), may hold values from -1.5 to 1.5
- right_state: float32 [131072], P(('dom', 'sub')), may hold values from 0.003 to 0.3
- rel_ops: bfloat16 [512, 256, 256], P('dom'), may hold values from -0.375 to 0.375
- left_ids: int32 [2, 262144], P(None, ('dom', 'sub')), may hold values from 0 to 511
- right_ids: int32 [2, 262144], P(None, ('dom', 'sub')), may hold values from 0 to 1023
- relations: int32 [2, 262144, 1], P(None, ('dom', 'sub')), may hold values from 0 to 511; in each aligned block of 512 rows (0 to 511, 512 to 1023, ..., all dimensions but the last counted through in order) at most 2 rows name the same one
- negatives: int32 [2, 1024, 1024], P(None, ('dom', 'sub')), may hold values from 0 to 1023
- live: int32 [2, 512], P(None, ('dom', 'sub')), may hold values from 128 to 512, as said below
Outputs:
- left_out: float32 [262144, 256], P(('dom', 'sub'))
- right_out: float32 [131072, 256], P(('dom', 'sub'))
- rel_grad: float32 [512, 256, 256], P('dom')
Inputs may be any that keep to these rules, and one draw needn't show every extreme that they name: `relations`: in one device's 512 rows of a round no relation is named more than 2 times. In every round some device has all 512 edges live.
All inputs are finite; a program needn't handle non-finite values.
Results may differ from a plain program's by a relative error of at most 0.015.
Values may be sent and summed in bfloat16 or wider, within the bound.
A program may use at most 64 MiB of HBM per device.

v0:
```python
import jax
import jax.numpy as jnp
from jax import lax
from jax.sharding import PartitionSpec as P

LEARNING_RATE = 0.1
STABILIZER = 1e-06


def shifted(shard, axis, by):
    count = lax.axis_size(axis)
    return lax.ppermute(shard, axis, [(i, (i + by) % count) for i in range(count)])


def adagrad(embedding, state, gradient):
    new_state = state + jnp.mean(gradient * gradient, axis=1)
    step_size = LEARNING_RATE / (jnp.sqrt(new_state) + STABILIZER)
    return (embedding - step_size[:, None] * gradient, new_state)


def slot_layout(relation_ids, capacity):
    count = relation_ids.shape[0]
    order = jnp.arange(count, dtype=jnp.int32)
    earlier = (relation_ids[:, None] == relation_ids[None, :]) & (order[:, None] > order[None, :])
    return relation_ids * capacity + jnp.sum(earlier.astype(jnp.int32), axis=1)


def to_slots(values, slot_ids, total_rel, capacity):
    width = values.shape[1]
    filled = jnp.zeros((total_rel * capacity, width), jnp.bfloat16).at[slot_ids].set(values)
    return filled.reshape(total_rel, capacity, width)


def per_device(
    left_emb,
    left_state,
    right_emb,
    right_state,
    rel_ops,
    left_ids,
    right_ids,
    relations,
    negatives,
    live,
):
    rel_local, width = (rel_ops.shape[0], rel_ops.shape[1])
    total_rel = rel_local * lax.axis_size("dom")
    edge_count = left_ids.shape[1]
    capacity = max(2, 2 * edge_count // total_rel)
    span_count, neg_count = (negatives.shape[1], negatives.shape[2])
    span_rows = edge_count // span_count
    rounds_total = left_ids.shape[0]
    rel_total = jnp.zeros((rel_local, width, width), jnp.float32)
    left_cur, left_st = (left_emb, left_state)
    right_cur, right_st = (right_emb, right_state)
    for bucket in range(rounds_total):
        final_round = bucket + 1 == rounds_total
        right_all = lax.all_gather(right_cur.astype(jnp.bfloat16), "sub", axis=0, tiled=True)
        relation_ids = relations[bucket, :, 0]
        slot_ids = slot_layout(relation_ids, capacity)
        left_rows = left_cur[left_ids[bucket]].astype(jnp.bfloat16)
        outbox = to_slots(left_rows, slot_ids, total_rel, capacity)
        inbox = lax.all_to_all(outbox, "dom", split_axis=0, concat_axis=1, tiled=True)
        mapped = jnp.einsum(
            "rsd,rde->rse", inbox, rel_ops, preferred_element_type=jnp.float32
        ).astype(jnp.bfloat16)
        returned = lax.all_to_all(mapped, "dom", split_axis=1, concat_axis=0, tiled=True)
        transformed = returned.reshape(total_rel * capacity, width)[slot_ids]
        pos_rows = right_all[right_ids[bucket]]
        neg_rows = right_all[negatives[bucket]]
        live_mask = (jnp.arange(edge_count, dtype=jnp.int32) < live[bucket, 0]).astype(jnp.float32)
        positive = jnp.sum(transformed.astype(jnp.float32) * pos_rows.astype(jnp.float32), axis=1)
        blocks = transformed.reshape(span_count, span_rows, width)
        scores = jnp.einsum("cid,cjd->cij", blocks, neg_rows, preferred_element_type=jnp.float32)
        pos_weight = -jax.nn.sigmoid(-positive) * live_mask
        neg_weight = (
            jax.nn.sigmoid(scores) * live_mask.reshape(span_count, span_rows, 1) / neg_count
        ).astype(jnp.bfloat16)
        neg_part = jnp.einsum(
            "cij,cjd->cid", neg_weight, neg_rows, preferred_element_type=jnp.float32
        )
        grad_mapped = (
            pos_weight[:, None] * pos_rows.astype(jnp.float32) + neg_part.reshape(edge_count, width)
        ).astype(jnp.bfloat16)
        grad_neg = jnp.einsum(
            "cij,cid->cjd", neg_weight, blocks, preferred_element_type=jnp.float32
        )
        partial_value = jnp.zeros((right_all.shape[0], width), jnp.float32)
        partial_value = partial_value.at[right_ids[bucket]].add(
            pos_weight[:, None] * transformed.astype(jnp.float32)
        )
        partial_value = partial_value.at[negatives[bucket].reshape(-1)].add(
            grad_neg.reshape(-1, width)
        )
        right_grad = lax.psum_scatter(
            partial_value.astype(jnp.bfloat16), "sub", scatter_dimension=0, tiled=True
        ).astype(jnp.float32)
        grad_box = to_slots(grad_mapped, slot_ids, total_rel, capacity)
        inbox_grad = lax.all_to_all(grad_box, "dom", split_axis=0, concat_axis=1, tiled=True)
        rel_term = jnp.einsum("rsd,rse->rde", inbox, inbox_grad, preferred_element_type=jnp.float32)
        input_grad = jnp.einsum(
            "rse,rde->rsd", inbox_grad, rel_ops, preferred_element_type=jnp.float32
        ).astype(jnp.bfloat16)
        grad_back = lax.all_to_all(input_grad, "dom", split_axis=1, concat_axis=0, tiled=True)
        left_grad_rows = grad_back.reshape(total_rel * capacity, width)[slot_ids].astype(
            jnp.float32
        )
        left_grad = (
            jnp.zeros((left_cur.shape[0], width), jnp.float32)
            .at[left_ids[bucket]]
            .add(left_grad_rows)
        )
        left_cur, left_st = adagrad(left_cur, left_st, left_grad)
        rel_total = rel_total + lax.psum(rel_term.astype(jnp.bfloat16), "sub").astype(jnp.float32)
        if final_round:
            right_cur, right_st = adagrad(right_cur, right_st, right_grad)
        else:
            updated_emb, updated_state = adagrad(right_cur, right_st, right_grad)
            right_cur, right_st = (
                shifted(updated_emb.astype(jnp.bfloat16), "dom", 1).astype(updated_emb.dtype),
                shifted(updated_state.astype(jnp.bfloat16), "dom", 1).astype(updated_state.dtype),
            )
    return (left_cur, right_cur, rel_total)


def solution(mesh):
    placed = (
        P(("dom", "sub"), None),
        P(("dom", "sub")),
        P(("dom", "sub"), None),
        P(("dom", "sub")),
        P("dom", None, None),
        P(None, ("dom", "sub")),
        P(None, ("dom", "sub")),
        P(None, ("dom", "sub"), None),
        P(None, ("dom", "sub"), None),
        P(None, ("dom", "sub")),
    )
    return jax.shard_map(
        per_device,
        mesh=mesh,
        in_specs=placed,
        out_specs=(P(("dom", "sub"), None), P(("dom", "sub"), None), P("dom", None, None)),
        check_vma=False,
    )
```

profile of v0, /device:TPU:1, one launch (start us, length us, event | category | flops | bytes accessed | tf_op | source)
XLA Modules:
  0.0 456.1 jit_solution(17377943576679363864)
XLA Ops:
  9.9 5.7 %scatter_custom_fusion = bf16[1024,256]{1,0:T(8,128)(2,1)S(1)} fusion(s32[512]{0:T(512)S(1)} %bitcast.155, bf16[]{:T(256)} %constant.16.clone.1, f32[512,256]{1,0:T(8,128)} %param.10, s32[1024]{0:T(1024)S(1)} %pad_clamp_fusion.5), kind=kCustom, calls=%fused_computation.75 | custom fusion | bytes 524800 | tf_op jit(solution)/shard_map/scatter | solution.py:30
  16.6 18.6 %all-to-all-start = ((bf16[512,2,256]{2,1,0:T(2,128)(2,1)}), bf16[512,2,256]{2,1,0:T(2,128)(2,1)S(1)}, u32[]{:S(2)}, u32[]{:S(2)}) async-start(bf16[512,2,256]{2,1,0:T(2,128)(2,1)} %reshape.378), calls=%async_computation | async-start | bytes 1048576 | tf_op jit(solution)/shard_map/all_to_all | solution.py:63
  35.8 17.1 %all-to-all-done = bf16[512,2,256]{2,1,0:T(2,128)(2,1)S(1)} async-done(((bf16[512,2,256]{2,1,0:T(2,128)(2,1)}), bf16[512,2,256]{2,1,0:T(2,128)(2,1)S(1)}, u32[]{:S(2)}, u32[]{:S(2)}) %all-to-all-start) | async-done | bytes 524320 | tf_op jit(solution)/shard_map/all_to_all | solution.py:63
  55.1 8.6 %all-to-all-start.1 = ((bf16[4,256,256]{2,0,1:T(4,128)(2,1)}), bf16[4,256,256]{2,0,1:T(4,128)(2,1)}, u32[]{:S(2)}, u32[]{:S(2)}) async-start(bf16[4,256,256]{2,0,1:T(4,128)(2,1)} %copy.50), calls=%async_computation.1 | async-start | bytes 1048576 | tf_op jit(solution)/shard_map/all_to_all | solution.py:67
  63.7 17.9 %all_gather.6 = bf16[1024,256]{1,0:T(8,128)(2,1)S(1)} all-gather(bf16[256,256]{1,0:T(8,128)(2,1)S(1)} %convert_element_type.116), channel_id=1, replica_groups=mesh['dom'=128,'sub'=4] {'sub'}, dimensions={0}, use_global_device_ids=true | all-gather | bytes 655360 | tf_op jit(solution)/shard_map/all_gather | solution.py:58
  83.6 7.5 %gather_fusion.2 = bf16[2048,256]{1,0:T(8,128)(2,1)S(1)} fusion(bf16[1024,256]{1,0:T(8,128)(2,1)S(1)} %all_gather.6, s32[2048]{0:T(1024)S(1)} %bitcast_clamp_fusion.1), kind=kCustom, calls=%fused_computation.3 | custom fusion | bytes 2105344 | tf_op jit(solution)/shard_map/gather | solution.py:70
  103.7 31.8 %all_to_all.132 = bf16[512,2,256]{2,1,0:T(2,128)(2,1)S(1)} all-to-all(bf16[512,2,256]{2,1,0:T(2,128)(2,1)S(1)} %reshape.382), channel_id=1, replica_groups=mesh['dom'=128,'sub'=4] {'dom'}, dimensions={0} | all-to-all | bytes 1048576 | tf_op jit(solution)/shard_map/all_to_all | solution.py:99
  137.7 8.0 %all-to-all-start.3 = ((bf16[4,256,256]{2,0,1:T(4,128)(2,1)}), bf16[4,256,256]{2,0,1:T(4,128)(2,1)S(1)}, u32[]{:S(2)}, u32[]{:S(2)}) async-start(bf16[4,256,256]{2,0,1:T(4,128)(2,1)} %copy.53), calls=%async_computation.3 | async-start | bytes 1048576 | tf_op jit(solution)/shard_map/all_to_all | solution.py:104
  145.7 17.7 %all-to-all-done.3 = bf16[4,256,256]{2,0,1:T(4,128)(2,1)S(1)} async-done(((bf16[4,256,256]{2,0,1:T(4,128)(2,1)}), bf16[4,256,256]{2,0,1:T(4,128)(2,1)S(1)}, u32[]{:S(2)}, u32[]{:S(2)}) %all-to-all-start.3) | async-done | bytes 524320 | tf_op jit(solution)/shard_map/all_to_all | solution.py:104
  164.1 4.9 %scatter_custom_fusion.2 = f32[512,256]{1,0:T(8,128)S(1)} fusion(s32[512]{0:T(512)S(1)} %bitcast.152, f32[]{:T(128)} %constant.13.clone.1, bf16[1024,256]{1,0:T(8,128)(2,1)S(1)} %reshape.383, s32[1024]{0:T(1024)S(1)} %pad_clamp_fusion.4), kind=kCustom, calls=%fused_computation.60 | custom fusion | flops 262144 | bytes 1052676 | tf_op jit(solution)/shard_map/scatter-add | solution.py:111
  170.3 4.0 scatter_custom_fusion.3
  175.4 7.9 %all-to-all-start.4 = ((bf16[512,2,256]{2,1,0:T(2,128)(2,1)}), bf16[512,2,256]{2,1,0:T(2,128)(2,1)S(1)}, u32[]{:S(2)}, u32[]{:S(2)}) async-start(bf16[512,2,256]{2,1,0:T(2,128)(2,1)} %reshape.384), calls=%async_computation.4 | async-start | bytes 1048576 | tf_op jit(solution)/shard_map/all_to_all | solution.py:63
  190.4 12.4 %scatter_fusion = f32[1024,256]{1,0:T(8,128)S(1)} fusion(f32[1024,256]{1,0:T(8,128)S(1)} %scatter_custom_fusion.4, s32[2048]{0:T(1024)S(1)} %bitcast.138, f32[2048,256]{1,0:T(8,128)} %bitcast.118), kind=kCustom, calls=%fused_computation.15 | custom fusion | flops 524288 | bytes 6299648 | tf_op jit(solution)/shard_map/scatter-add | solution.py:92
  205.8 13.6 %all-to-all-start.5 = ((bf16[4,256,256]{2,0,1:T(4,128)(2,1)}), bf16[4,256,256]{2,0,1:T(4,128)(2,1)S(1)}, u32[]{:S(2)}, u32[]{:S(2)}) async-start(bf16[4,256,256]{2,0,1:T(4,128)(2,1)} %copy.56), calls=%async_computation.5 | async-start | bytes 1048576 | tf_op jit(solution)/shard_map/all_to_all | solution.py:67
  219.9 27.8 %reduce-scatter.3.cloned.1.call-done = bf16[256,256]{1,0:T(8,128)(2,1)} async-done(((bf16[1024,256]{1,0:T(8,128)(2,1)}), bf16[256,256]{1,0:T(8,128)(2,1)}) %reduce-scatter.3.cloned.1.call-update) | async-done | bytes 131088 | tf_op jit(solution)/shard_map/reduce_scatter | solution.py:95
  254.0 8.6 %collective-permute-done = bf16[256,256]{1,0:T(8,128)(2,1)S(1)} collective-permute-done((bf16[256,256]{1,0:T(8,128)(2,1)S(1)}, bf16[256,256]{1,0:T(8,128)(2,1)S(1)}, u32[]{:S(2)}, u32[]{:S(2)}) %collective-permute-start) | collective-permute-done | bytes 131104 | tf_op jit(solution)/shard_map/ppermute | solution.py:12
  262.6 12.0 %all_gather.7 = bf16[1024,256]{1,0:T(8,128)(2,1)S(1)} all-gather(bf16[256,256]{1,0:T(8,128)(2,1)S(1)} %collective-permute-done), channel_id=1, replica_groups=mesh['dom'=128,'sub'=4] {'sub'}, dimensions={0}, use_global_device_ids=true | all-gather | bytes 655360 | tf_op jit(solution)/shard_map/all_gather | solution.py:58
  276.7 9.1 %gather_fusion.5 = bf16[2048,256]{1,0:T(8,128)(2,1)} fusion(bf16[1024,256]{1,0:T(8,128)(2,1)S(1)} %all_gather.7, s32[2048]{0:T(1024)S(1)} %bitcast_clamp_fusion), kind=kCustom, calls=%fused_computation.8 | custom fusion | bytes 2105344 | tf_op jit(solution)/shard_map/gather | solution.py:70
  298.7 8.8 %all-to-all-start.6 = ((bf16[512,2,256]{2,1,0:T(2,128)(2,1)}), bf16[512,2,256]{2,1,0:T(2,128)(2,1)}, u32[]{:S(2)}, u32[]{:S(2)}) async-start(bf16[512,2,256]{2,1,0:T(2,128)(2,1)} %reshape.389), calls=%async_computation.7 | async-start | bytes 1048576 | tf_op jit(solution)/shard_map/all_to_all | solution.py:99
  314.6 12.6 %scatter_fusion.1 = f32[1024,256]{1,0:T(8,128)S(1)} fusion(f32[1024,256]{1,0:T(8,128)S(1)} %scatter_custom_fusion.8, s32[2048]{0:T(1024)S(1)} %bitcast.139, f32[2048,256]{1,0:T(8,128)} %bitcast.119), kind=kCustom, calls=%fused_computation.19 | custom fusion | flops 524288 | bytes 6299648 | tf_op jit(solution)/shard_map/scatter-add | solution.py:92
  331.2 13.5 %all-to-all-start.7 = ((bf16[4,256,256]{2,0,1:T(4,128)(2,1)}), bf16[4,256,256]{2,0,1:T(4,128)(2,1)S(1)}, u32[]{:S(2)}, u32[]{:S(2)}) async-start(bf16[4,256,256]{2,0,1:T(4,128)(2,1)} %copy.60), calls=%async_computation.8 | async-start | bytes 1048576 | tf_op jit(solution)/shard_map/all_to_all | solution.py:104
  349.6 21.5 %reduce-scatter.5.cloned.1.call-done = bf16[256,256]{1,0:T(8,128)(2,1)} async-done(((bf16[1024,256]{1,0:T(8,128)(2,1)}), bf16[256,256]{1,0:T(8,128)(2,1)}) %reduce-scatter.5.cloned.1.call-update) | async-done | bytes 131088 | tf_op jit(solution)/shard_map/reduce_scatter | solution.py:95
  374.6 5.0 %scatter_custom_fusion.7 = f32[512,256]{1,0:T(8,128)S(1)} fusion(s32[512]{0:T(512)} %bitcast.145, f32[]{:T(128)} %constant.13.clone.1, bf16[1024,256]{1,0:T(8,128)(2,1)S(1)} %reshape.390, s32[1024]{0:T(1024)S(1)} %copy-done.11), kind=kCustom, calls=%fused_computation.54 | custom fusion | flops 262144 | bytes 1053184 | tf_op jit(solution)/shard_map/scatter-add | solution.py:111
  380.7 66.1 %all-reduce.3.cloned.1.call-done = (bf16[4,256,256]{2,1,0:T(8,128)(2,1)}, bf16[4,256,256]{2,1,0:T(8,128)(2,1)}) async-done(((bf16[4,256,256]{2,1,0:T(8,128)(2,1)}, bf16[4,256,256]{2,1,0:T(8,128)(2,1)}), (bf16[4,256,256]{2,1,0:T(8,128)(2,1)}, bf16[4,256,256]{2,1,0:T(8,128)(2,1)})) %all-reduce.3.cloned.1.call-update) | async-done | bytes 1048592 | tf_op jit(solution)/shard_map/psum | solution.py:114
  (149 shorter events, 80.4 us)
Async XLA Ops:
  7.2 46.4 %copy-start = (bf16[4,256,256]{2,1,0:T(8,128)(2,1)S(1)}, bf16[4,256,256]{2,1,0:T(8,128)(2,1)}, u32[]{:S(2)}) copy-start(bf16[4,256,256]{2,1,0:T(8,128)(2,1)} %param.14) | copy-start | bytes 1572868
  7.2 28.0 %copy-start.8 = (f32[256,256]{1,0:T(8,128)S(1)}, f32[256,256]{1,0:T(8,128)}, u32[]{:S(2)}) copy-start(f32[256,256]{1,0:T(8,128)} %param.12) | copy-start | bytes 786436
  7.2 28.1 %copy-start.19 = (s32[2,512]{1,0:T(2,128)S(1)}, s32[2,512]{1,0:T(2,128)}, u32[]{:S(2)}) copy-start(s32[2,512]{1,0:T(2,128)} %param.16) | copy-start | bytes 12292
  8.0 137.7 %copy-start.16 = (s32[512,1]{0,1:T(1,128)}, s32[512,1]{0,1:T(1,128)S(1)}, u32[]{:S(2)}) copy-start(s32[512,1]{0,1:T(1,128)S(1)} %get-tuple-element.15) | copy-start | bytes 6148
  9.9 209.4 %copy-start.18 = (s32[512,1]{0,1:T(1,128)}, s32[512,1]{0,1:T(1,128)S(1)}, u32[]{:S(2)}) copy-start(s32[512,1]{0,1:T(1,128)S(1)} %get-tuple-element.11) | copy-start | bytes 6148
  16.6 36.4 %all-to-all-start = ((bf16[512,2,256]{2,1,0:T(2,128)(2,1)}), bf16[512,2,256]{2,1,0:T(2,128)(2,1)S(1)}, u32[]{:S(2)}, u32[]{:S(2)}) async-start(bf16[512,2,256]{2,1,0:T(2,128)(2,1)} %reshape.378), calls=%async_computation | async-start | bytes 1048576 | tf_op jit(solution)/shard_map/all_to_all | solution.py:63
  55.1 28.5 %copy-start.10 = (s32[2,2,1024]{2,1,0:T(2,128)S(1)}, s32[2,2,1024]{2,1,0:T(2,128)}, u32[]{:S(2)}) copy-start(s32[2,2,1024]{2,1,0:T(2,128)} %param.18) | copy-start | bytes 49156
  55.1 37.3 %all-to-all-start.1 = ((bf16[4,256,256]{2,0,1:T(4,128)(2,1)}), bf16[4,256,256]{2,0,1:T(4,128)(2,1)}, u32[]{:S(2)}, u32[]{:S(2)}) async-start(bf16[4,256,256]{2,0,1:T(4,128)(2,1)} %copy.50), calls=%async_computation.1 | async-start | bytes 1048576 | tf_op jit(solution)/shard_map/all_to_all | solution.py:67
  137.7 25.8 %all-to-all-start.3 = ((bf16[4,256,256]{2,0,1:T(4,128)(2,1)}), bf16[4,256,256]{2,0,1:T(4,128)(2,1)S(1)}, u32[]{:S(2)}, u32[]{:S(2)}) async-start(bf16[4,256,256]{2,0,1:T(4,128)(2,1)} %copy.53), calls=%async_computation.3 | async-start | bytes 1048576 | tf_op jit(solution)/shard_map/all_to_all | solution.py:104
  145.7 23.5 %copy-start.14 = (f32[512]{0:T(512)S(1)}, f32[512]{0:T(512)}, u32[]{:S(2)}) copy-start(f32[512]{0:T(512)} %param.11) | copy-start | bytes 6148
  175.4 28.2 %all-to-all-start.4 = ((bf16[512,2,256]{2,1,0:T(2,128)(2,1)}), bf16[512,2,256]{2,1,0:T(2,128)(2,1)S(1)}, u32[]{:S(2)}, u32[]{:S(2)}) async-start(bf16[512,2,256]{2,1,0:T(2,128)(2,1)} %reshape.384), calls=%async_computation.4 | async-start | bytes 1048576 | tf_op jit(solution)/shard_map/all_to_all | solution.py:63
  183.3 64.4 %reduce-scatter.3.cloned.1.call-start = ((), (), s32[]{:S(2)}) async-start(), calls=%async_computation.10 | async-start | bytes 655360 | tf_op jit(solution)/shard_map/reduce_scatter | solution.py:95
  204.2 44.5 %copy-start.21 = (f32[256]{0:T(256)S(1)}, f32[256]{0:T(256)}, u32[]{:S(2)}) copy-start(f32[256]{0:T(256)} %param.13) | copy-start | bytes 3076
  204.2 45.1 %copy-start.9 = (f32[256,256]{1,0:T(8,128)S(1)}, f32[256,256]{1,0:T(8,128)}, u32[]{:S(2)}) copy-start(f32[256,256]{1,0:T(8,128)} %param.12) | copy-start | bytes 786436
  204.2 49.2 %copy-start.17 = (s32[512,1]{0,1:T(1,128)S(1)}, s32[512,1]{0,1:T(1,128)}, u32[]{:S(2)}) copy-start(s32[512,1]{0,1:T(1,128)} %get-tuple-element.9) | copy-start | bytes 6148
  205.8 80.0 %all-to-all-start.5 = ((bf16[4,256,256]{2,0,1:T(4,128)(2,1)}), bf16[4,256,256]{2,0,1:T(4,128)(2,1)S(1)}, u32[]{:S(2)}, u32[]{:S(2)}) async-start(bf16[4,256,256]{2,0,1:T(4,128)(2,1)} %copy.56), calls=%async_computation.5 | async-start | bytes 1048576 | tf_op jit(solution)/shard_map/all_to_all | solution.py:67
  250.3 12.3 %collective-permute-start = (bf16[256,256]{1,0:T(8,128)(2,1)S(1)}, bf16[256,256]{1,0:T(8,128)(2,1)S(1)}, u32[]{:S(2)}, u32[]{:S(2)}) collective-permute-start(bf16[256,256]{1,0:T(8,128)(2,1)S(1)} %fusion.18), channel_id=1, source_target_pairs={{0,4},{4,8},{8,12},{12,16},{16,20},{20,24},{24,28},{28,32},{32,36}... | collective-permute-start | bytes 393224 | tf_op jit(solution)/shard_map/ppermute | solution.py:12
  276.7 13.5 %copy-start.4 = (bf16[512,256]{1,0:T(8,128)(2,1)}, bf16[512,256]{1,0:T(8,128)(2,1)S(1)}, u32[]{:S(2)}) copy-start(bf16[512,256]{1,0:T(8,128)(2,1)S(1)} %gather_fusion.4) | copy-start | bytes 786436
  298.7 29.3 %all-to-all-start.6 = ((bf16[512,2,256]{2,1,0:T(2,128)(2,1)}), bf16[512,2,256]{2,1,0:T(2,128)(2,1)}, u32[]{:S(2)}, u32[]{:S(2)}) async-start(bf16[512,2,256]{2,1,0:T(2,128)(2,1)} %reshape.389), calls=%async_computation.7 | async-start | bytes 1048576 | tf_op jit(solution)/shard_map/all_to_all | solution.py:99
  307.5 63.6 %reduce-scatter.5.cloned.1.call-start = ((), (), s32[]{:S(2)}) async-start(), calls=%async_computation.11 | async-start | bytes 655360 | tf_op jit(solution)/shard_map/reduce_scatter | solution.py:95
  330.0 15.9 %copy-start.22 = (bf16[256]{0:T(256)(128)(2,1)S(1)}, bf16[256]{0:T(256)(128)(2,1)}, u32[]{:S(2)}) copy-start(bf16[256]{0:T(256)(128)(2,1)} %get-tuple-element.17) | copy-start | bytes 1540
  331.2 42.7 %all-to-all-start.7 = ((bf16[4,256,256]{2,0,1:T(4,128)(2,1)}), bf16[4,256,256]{2,0,1:T(4,128)(2,1)S(1)}, u32[]{:S(2)}, u32[]{:S(2)}) async-start(bf16[4,256,256]{2,0,1:T(4,128)(2,1)} %copy.60), calls=%async_computation.8 | async-start | bytes 1048576 | tf_op jit(solution)/shard_map/all_to_all | solution.py:104
  344.8 102.0 %all-reduce.3.cloned.1.call-start = ((), (), s32[]{:S(2)}) async-start(), calls=%async_computation.12 | async-start | bytes 2097152 | tf_op jit(solution)/shard_map/psum | solution.py:114
  346.0 26.1 %collective-permute-start.1 = (bf16[256]{0:T(256)(128)(2,1)S(1)}, bf16[256]{0:T(256)(128)(2,1)S(1)}, u32[]{:S(2)}, u32[]{:S(2)}) collective-permute-start(bf16[256]{0:T(256)(128)(2,1)S(1)} %copy-done.22), channel_id=1, source_target_pairs={{0,4},{4,8},{8,12},{12,16},{16,20},{20,24},{24,28},{28,32},{32,36}... | collective-permute-start | bytes 1544 | tf_op jit(solution)/shard_map/ppermute | solution.py:12
  (11 other events, 58.2 us)
Sparse Core Ops, SparseCore 0:
  203.7 43.9 reduce-scatter.2
  328.2 42.8 reduce-scatter.4
  374.1 72.6 all-reduce.2
where the time goes:
time: 465 us; the launch traced here: 456 us
  waiting for transfers between devices  159 us (34%)
  starting transfers between devices  83.7 us (18%)
  other arithmetic  61.7 us (13%)
  blocking collectives  61.7 us (13%)
  local copies, waits for them, and re-layouts  61.6 us (13%)
  between operations  15 us (3%)
  matrix products  13.5 us (3%)
    psum x1, waiting for transfers between devices, per_device(): lax.psum(rel_term.astype(jnp.bfloat16), 'sub').astype(jnp.float32)  66.1 us
    reduce_scatter x2, waiting for transfers between devices, per_device(): lax.psum_scatter(partial_value.astype(jnp.bfloat16), 'sub', scatter_dimen...  49.3 us
    all_to_all x1, blocking collectives, per_device(): lax.all_to_all(grad_box, 'dom', split_axis=0, concat_axis=1, tiled=True)  31.8 us
    all_gather x2, blocking collectives, per_device(): lax.all_gather(right_cur.astype(jnp.bfloat16), 'sub', axis=0, tiled=True)  29.9 us
    all_to_all x2, starting transfers between devices, per_device(): lax.all_to_all(outbox, 'dom', split_axis=0, concat_axis=1, tiled=True)  26.5 us
    scatter-add x2, other arithmetic, per_device(): partial_value.at[negatives[bucket].reshape(-1)]  25 us
    all_to_all x2, starting transfers between devices, per_device(): lax.all_to_all(mapped, 'dom', split_axis=1, concat_axis=0, tiled=True)  22.2 us
    all_to_all x2, starting transfers between devices, per_device(): lax.all_to_all(input_grad, 'dom', split_axis=1, concat_axis=0, tiled=True)  21.5 us
  transfers between devices with their start and end apart: 12, of which 6 were waited for; matrix products, arithmetic and copies ran while one was open for 19% of the time, Pallas kernels for 0%

commit v1 on v0

v1 whole, which is shorter than its diff:
```python
import jax
import jax.numpy as jnp
from jax import lax
from jax.experimental import pallas as pl
from jax.experimental.pallas import tpu as pltpu
from jax.sharding import PartitionSpec as P

LEARNING_RATE = 0.1
STABILIZER = 1e-06
MESH = pl.DeviceIdType.MESH
F32 = jnp.float32
BF16 = jnp.bfloat16
NX, NY, NZ = 4, 4, 8
DOM = NX * NY * NZ
WIDTH = 256
EDGES = 512
SLOTS = 1024
ROWS = 512
BLOCK = 1024
PART = 256
NEG = 1024


def dot(a, b):
    return lax.dot_general(a, b, (((1,), (0,)), ((), ())), preferred_element_type=F32)


def dot_bt(a, b):
    return lax.dot_general(a, b, (((1,), (1,)), ((), ())), preferred_element_type=F32)


def dot_at(a, b):
    return lax.dot_general(a, b, (((0,), (0,)), ((), ())), preferred_element_type=F32)


def iota(shape, dim):
    return lax.broadcasted_iota(jnp.int32, shape, dim)


def onehot(hit):
    return jnp.where(hit, 1.0, 0.0).astype(BF16)


def pack(rows):
    n = rows.shape[0] // 8
    low = rows[:, :128].reshape(n, 8, 128)
    high = rows[:, 128:].reshape(n, 8, 128)
    return jnp.concatenate([low, high], axis=1).astype(BF16)


def unpack(chunks):
    n = chunks.shape[0]
    wide = chunks.astype(F32)
    low = wide[:, :8].reshape(n * 8, 128)
    high = wide[:, 8:].reshape(n * 8, 128)
    return jnp.concatenate([low, high], axis=1)


def place():
    me = lax.axis_index("dom")
    sub = lax.axis_index("sub")
    return me // (NY * NZ), (me // NZ) % NY, me % NZ, sub // 2, sub % 2


def each_partner(visit):
    mx, my, mz, yh, core = place()
    for dy in range(NY):
        qy = lax.rem(my + dy, NY)
        if dy == 0:
            flip = 0
        elif dy == 1:
            flip = jnp.where(my == NY - 1, 1, 0)
        elif dy == NY - 1:
            flip = jnp.where(my == 0, 1, 0)
        else:
            flip = core
        sub = lax.rem(yh + flip, 2) * 2 + core

        def plane(dx, first):
            base = (lax.rem(mx + dx, NX) * NY + qy) * NZ
            for dz in range(NZ):
                if not (first and dz == 0):
                    q = base + lax.rem(mz + dz, NZ)
                    visit(q, (q, sub))

        def body(dx, carry):
            plane(dx, False)
            return carry

        if dy == 0:
            plane(0, True)
            lax.fori_loop(1, NX, body, 0)
        else:
            lax.fori_loop(0, NX, body, 0)


def kernel(
    left_ref, lstate_ref, right_ref, rstate_ref, rel_ref, lids_ref, rids_ref, rels_ref, negs_ref, live_ref,
    left_out, right_out, rel_out,
    send, recv, to_slot, from_slot, row_slot, slot_row, ids, counts, rel_t, inbox, masked, moved, edge_grad, weights,
    blk, part, part_in, lstate, rstate, shift_e, shift_e_in, shift_s, shift_s_in, rel_acc, rel_send, rel_in,
    a2a_s, a2a_r, gat_s, gat_r, red_s, red_r, shf_s, shf_r, rel_s, rel_r,
):
    me = lax.axis_index("dom")
    sub = lax.axis_index("sub")
    core = lax.rem(sub, 2)
    following = (lax.rem(me + 1, DOM), sub)
    previous = (lax.rem(me + DOM - 1, DOM), sub)
    relatives = [(me, lax.rem(sub // 2 + o // 2, 2) * 2 + lax.rem(core + o % 2, 2)) for o in (1, 2, 3)]

    barrier = pltpu.get_barrier_semaphore()

    def greet(q, device):
        pl.semaphore_signal(barrier, inc=1, device_id=device, device_id_type=MESH)

    each_partner(greet)
    for device in relatives + [following, previous]:
        greet(None, device)

    def remote(src, dst, send_sem, recv_sem, device):
        return pltpu.make_async_remote_copy(
            src_ref=src, dst_ref=dst, send_sem=send_sem, recv_sem=recv_sem, device_id=device, device_id_type=MESH
        )

    def blocks(count, body):
        def step(i, carry):
            body(i)
            return carry

        lax.fori_loop(0, count, step, 0)

    def exchange(k):
        def start(q, device):
            remote(send.at[k % 2, q], recv.at[k, me], a2a_s.at[k], a2a_r.at[k], device).start()

        each_partner(start)
        recv[k, me] = send[k % 2, me]

    def sent(k):
        most = send.at[k % 2, pl.ds(0, DOM - 1)]
        pltpu.make_async_copy(most, most, a2a_s.at[k]).wait()

    def arrived(k):
        most = recv.at[k, pl.ds(0, DOM - 1)]
        pltpu.make_async_copy(most, most, a2a_r.at[k]).wait()

    rows = jnp.concatenate(
        [rels_ref[...].astype(F32), lids_ref[...].astype(F32), rids_ref[...].astype(F32), lstate_ref[...],
         jnp.zeros((1, EDGES), F32)], axis=0)
    ids[...] = jnp.transpose(rows)
    lstate[...] = ids[:, 6:7]
    rstate[...] = jnp.transpose(jnp.broadcast_to(rstate_ref[...], (8, PART)))[:, 0:1]

    def index_work(r, stage):
        if stage == 0:
            rel_row = rels_ref[r : r + 1, :].astype(F32)
            rel_col = ids[:, r : r + 1]
            same = rel_row == rel_col
            lane, line = iota((EDGES, EDGES), 1), iota((EDGES, EDGES), 0)
            row_rank = jnp.sum(jnp.where(same & (line < lane), 1.0, 0.0), axis=0, keepdims=True)
            col_rank = jnp.sum(jnp.where(same & (lane < line), 1.0, 0.0), axis=1, keepdims=True)
            ids[:, 7:8] = 2.0 * rel_col + col_rank
            row_ids = (2.0 * rel_row + row_rank).astype(jnp.int32)
            gather = onehot(iota((EDGES, ROWS), 1) == ids[:, 2 + r : 3 + r].astype(jnp.int32))

            def fill(i):
                place_of = onehot(iota((256, EDGES), 0) + i * 256 == row_ids)
                to_slot[r, pl.ds(i * 256, 256), :] = place_of
                slot_row[r, pl.ds(i * 256, 256), :] = dot(place_of, gather).astype(BF16)

            blocks(4, fill)
        else:
            slot = ids[:, 7:8].astype(jnp.int32)
            for i in range(4):
                from_slot[r, :, i * 256 : (i + 1) * 256] = onehot(iota((EDGES, 256), 1) + i * 256 == slot)
            scatter = onehot(iota((ROWS, EDGES), 0) == lids_ref[r : r + 1, :])
            for i in range(4):
                row_slot[r, :, i * 256 : (i + 1) * 256] = dot(scatter, from_slot[r, :, i * 256 : (i + 1) * 256]).astype(BF16)
            for c in range(2):
                named = negs_ref[r, c : c + 1, :]
                high = onehot(iota((16, NEG), 0) == named // 128)
                low = onehot(iota((128, NEG), 0) == named % 128)
                tally = dot_bt(high, low)
                counts[2 * r + c : 2 * r + c + 1, :] = (
                    jnp.concatenate([tally[i : i + 1, :] for i in range(8)], axis=1) * (1.0 / NEG))

    def fill_outbox(k, table, r, values):
        def fill(i):
            send[k % 2, pl.ds(i * 32, 32)] = pack(dot(table[r, pl.ds(i * 256, 256), :], values))

        blocks(4, fill)

    def keep(o):
        return (iota((256, WIDTH), 0) % 8) // 2 == o

    def adagrad(value, state, gradient):
        state = state + jnp.mean(gradient * gradient, axis=1, keepdims=True)
        return value - LEARNING_RATE / (jnp.sqrt(state) + STABILIZER) * gradient, state

    def gather_block(r):
        for o in range(3):
            remote(blk.at[r, sub], blk.at[r, sub], gat_s.at[r, o], gat_r.at[r, o], relatives[o]).start()

    index_work(0, 0)
    left_out[...] = left_ref[...]
    fill_outbox(0, slot_row, 0, left_out[...].astype(BF16))
    blk[0, sub] = right_ref[...].astype(BF16)
    pl.semaphore_wait(barrier, DOM - 1 + 5)

    for r in range(2):
        k = 4 * r
        exchange(k)
        if r == 0:
            gather_block(0)
            index_work(0, 1)
            for o in range(4):
                rel_t[o] = jnp.transpose(rel_ref[o].astype(F32)).astype(BF16)
            right_now = right_ref
        else:
            for copy in shifts:
                copy.wait_recv()
            blk[1, sub] = shift_e_in[...]
            gather_block(1)
            rstate[...] = jnp.transpose(shift_s_in[...])[:, 0:1]
            right_now = shift_e_in
        arrived(k)
        if r == 1:
            sent(k - 1)

        def forward(i):
            row = unpack(recv[k, pl.ds(i * 32, 32)])
            inbox[r, pl.ds(i * 256, 256), :] = row.astype(BF16)
            mapped = sum(dot(jnp.where(keep(o), row, 0.0).astype(BF16), rel_ref[o]) for o in range(4))
            send[(k + 1) % 2, pl.ds(i * 32, 32)] = pack(mapped)

        blocks(4, forward)
        exchange(k + 1)
        if r == 0:
            index_work(1, 0)
            index_work(1, 1)
        arrived(k + 1)

        def settle(i):
            row = unpack(recv[k + 1, pl.ds(i * 32, 32)])
            inbox[2, pl.ds(i * 256, 256), :] = row.astype(BF16)

        blocks(4, settle)
        moved[...] = dot(from_slot[r], inbox[2]).astype(BF16)
        for o in range(3):
            remote(blk.at[r, sub], blk.at[r, sub], gat_s.at[r, o], gat_r.at[r, o], relatives[o]).wait()

        live = live_ref[r : r + 1, :]

        def score(i):
            at = pl.ds(i * 128, 128)
            y = moved[at, :]
            scores = jnp.concatenate([dot_bt(y, blk[r, j]) for j in range(4)], axis=1)
            mask = jnp.where(iota((128, 1), 0) + i * 128 < live, 1.0, 0.0)
            named = iota((128, BLOCK), 1) == ids[at, 4 + r : 5 + r].astype(jnp.int32)
            positive = jnp.sum(jnp.where(named, scores, 0.0), axis=1, keepdims=True)
            pull = -jax.nn.sigmoid(-positive) * mask
            push = jax.nn.sigmoid(scores) * counts[pl.ds(2 * r + i // 2, 1), :] * mask
            weight = (push + jnp.where(named, pull, 0.0)).astype(BF16)
            weights[at, :] = weight
            grad = sum(dot(weight[:, j * 256 : (j + 1) * 256], blk[r, j]) for j in range(4))
            edge_grad[at, :] = grad.astype(BF16)

        blocks(4, score)
        sent(k)
        fill_outbox(k + 2, to_slot, r, edge_grad[...])
        exchange(k + 2)
        for j in range(4):
            part[r, j] = dot_at(weights[:, j * 256 : (j + 1) * 256], moved[...]).astype(BF16)
        for o in range(3):
            remote(part.at[r, relatives[o][1]], part_in.at[r, o], red_s.at[r, o], red_r.at[r, o], relatives[o]).start()
        arrived(k + 2)
        sent(k + 1)

        def backward(i):
            row = unpack(recv[k + 2, pl.ds(i * 32, 32)])
            total = jnp.zeros((256, WIDTH), F32)
            for o in range(4):
                kept = jnp.where(keep(o), row, 0.0).astype(BF16)
                masked[o, pl.ds(i * 256, 256), :] = kept
                total = total + dot(kept, rel_t[o])
            send[(k + 3) % 2, pl.ds(i * 32, 32)] = pack(total)

        blocks(4, backward)
        exchange(k + 3)
        for o in range(4):
            term = dot_at(inbox[r], masked[o])
            rel_acc[o] = term if r == 0 else rel_acc[o] + term
        if r == 1:
            for o in range(4):
                rel_send[0, o] = rel_acc[o].astype(BF16)
            pair = [remote(rel_send.at[0, pl.ds(2 - 2 * core, 2)], rel_in.at[0], rel_s.at[0], rel_r.at[0], relatives[0])]
            pair[0].start()
        for o in range(3):
            remote(part.at[r, relatives[o][1]], part_in.at[r, o], red_s.at[r, o], red_r.at[r, o], relatives[o]).wait()
        gradient = part[r, sub].astype(F32)
        for o in range(3):
            gradient = gradient + part_in[r, o].astype(F32)
        value, state = adagrad(right_now[...].astype(F32), rstate[...], gradient)
        if r == 0:
            shift_e[...] = value.astype(BF16)
            shift_s[...] = jnp.transpose(jnp.broadcast_to(state, (PART, 128)))[0:8, :]
            shifts = [
                remote(shift_e, shift_e_in, shf_s.at[0], shf_r.at[0], following),
                remote(shift_s, shift_s_in, shf_s.at[1], shf_r.at[1], following),
            ]
            for copy in shifts:
                copy.start()
        else:
            right_out[...] = value
            pair[0].wait()
            for o in range(2):
                rel_send[1, o] = (rel_acc[2 * core + o] + rel_in[0, o].astype(F32)).astype(BF16)
            across = remote(rel_send.at[1, pl.ds(0, 2)], rel_in.at[1], rel_s.at[1], rel_r.at[1], relatives[1])
            across.start()
        arrived(k + 3)
        sent(k + 2)

        def settle_back(i):
            row = unpack(recv[k + 3, pl.ds(i * 32, 32)])
            inbox[2, pl.ds(i * 256, 256), :] = row.astype(BF16)

        blocks(4, settle_back)

        def update(i):
            at = pl.ds(i * 128, 128)
            value, state = adagrad(left_out[at, :], lstate[at, :], dot(row_slot[r, at, :], inbox[2]))
            left_out[at, :] = value
            lstate[at, :] = state

        blocks(4, update)
        if r == 0:
            fill_outbox(k + 4, slot_row, 1, left_out[...].astype(BF16))
    across.wait()
    for o in range(2):
        rel_send[2, o] = (rel_send[1, o].astype(F32) + rel_in[1, o].astype(F32)).astype(BF16)
    back = remote(rel_send.at[2, pl.ds(0, 2)], rel_in.at[2], rel_s.at[2], rel_r.at[2], relatives[0])
    back.start()
    for o in range(2):
        rel_out[2 * core + o] = rel_send[2, o].astype(F32)
    back.wait()
    for o in range(2):
        rel_out[2 - 2 * core + o] = rel_in[2, o].astype(F32)
    for copy in shifts:
        copy.wait_send()
    sent(7)


def per_device(left_emb, left_state, right_emb, right_state, rel_ops, left_ids, right_ids, relations, negatives, live):
    vmem = pltpu.VMEM
    dma = pltpu.SemaphoreType.DMA
    whole = pl.BlockSpec(memory_space=pltpu.VMEM)
    return pl.pallas_call(
        kernel,
        out_shape=(
            jax.ShapeDtypeStruct((ROWS, WIDTH), F32),
            jax.ShapeDtypeStruct((PART, WIDTH), F32),
            jax.ShapeDtypeStruct((4, WIDTH, WIDTH), F32),
        ),
        in_specs=[whole] * 10,
        out_specs=[whole] * 3,
        scratch_shapes=[
            vmem((2, DOM, 16, 128), BF16),
            vmem((8, DOM, 16, 128), BF16),
            vmem((2, SLOTS, EDGES), BF16),
            vmem((2, EDGES, SLOTS), BF16),
            vmem((2, ROWS, SLOTS), BF16),
            vmem((2, SLOTS, ROWS), BF16),
            vmem((EDGES, 8), F32),
            vmem((8, BLOCK), F32),
            vmem((4, WIDTH, WIDTH), BF16),
            vmem((3, SLOTS, WIDTH), BF16),
            vmem((4, SLOTS, WIDTH), BF16),
            vmem((EDGES, WIDTH), BF16),
            vmem((EDGES, WIDTH), BF16),
            vmem((EDGES, BLOCK), BF16),
            vmem((2, 4, PART, WIDTH), BF16),
            vmem((2, 4, PART, WIDTH), BF16),
            vmem((2, 3, PART, WIDTH), BF16),
            vmem((ROWS, 1), F32),
            vmem((PART, 1), F32),
            vmem((PART, WIDTH), BF16),
            vmem((PART, WIDTH), BF16),
            vmem((8, PART), F32),
            vmem((8, PART), F32),
            vmem((4, WIDTH, WIDTH), F32),
            vmem((3, 4, WIDTH, WIDTH), BF16),
            vmem((3, 2, WIDTH, WIDTH), BF16),
            dma((8,)), dma((8,)), dma((2, 3)), dma((2, 3)), dma((2, 3)), dma((2, 3)),
            dma((2,)), dma((2,)), dma((3,)), dma((3,)),
        ],
        compiler_params=pltpu.CompilerParams(collective_id=0, has_side_effects=True, vmem_limit_bytes=50 << 20),
    )(
        left_emb, left_state.reshape(1, -1), right_emb, right_state.reshape(1, -1), rel_ops, left_ids, right_ids,
        relations.reshape(2, -1), negatives, live,
    )


def solution(mesh):
    placed = (
        P(("dom", "sub"), None),
        P(("dom", "sub")),
        P(("dom", "sub"), None),
        P(("dom", "sub")),
        P("dom", None, None),
        P(None, ("dom", "sub")),
        P(None, ("dom", "sub")),
        P(None, ("dom", "sub"), None),
        P(None, ("dom", "sub"), None),
        P(None, ("dom", "sub")),
    )
    return jax.shard_map(
        per_device,
        mesh=mesh,
        in_specs=placed,
        out_specs=(P(("dom", "sub"), None), P(("dom", "sub"), None), P("dom", None, None)),
        check_vma=False,
    )
```

time: 465 us -> 190 us (0.41); the launches traced: 456 us -> 190 us
  Pallas kernels: 0 us -> 181 us
  waiting for transfers between devices: 159 us -> 0 us
  starting transfers between devices: 83.7 us -> 0 us
  other arithmetic: 61.7 us -> 0 us
  blocking collectives: 61.7 us -> 0 us
  local copies, waits for them, and re-layouts: 61.6 us -> 7.66 us
  between operations: 15 us -> 0.69 us
  matrix products: 13.5 us -> 0 us
    pallas_call x0 -> x1, Pallas kernels: none -> 181 us  [per_device(): pl.pallas_call(kernel, out_shape=(jax.ShapeDtypeStruct((ROWS, WIDTH), F32...]
    all_to_all x7 -> x0, starting transfers between devices: 79 us -> none  [the longest x2 26.5 us: per_device(): lax.all_to_all(outbox, 'dom', split_axis=0, concat_axis=1, tiled=True)]
    psum x1 -> x0, waiting for transfers between devices: 66.1 us -> none  [per_device(): lax.psum(rel_term.astype(jnp.bfloat16), 'sub').astype(jnp.float32)]
    reduce_scatter x2 -> x0, waiting for transfers between devices: 49.3 us -> none  [per_device(): lax.psum_scatter(partial_value.astype(jnp.bfloat16), 'sub', scatter_dimen...]
    scatter-add x6 -> x0, other arithmetic: 42.4 us -> none  [the longest x2 25 us: per_device(): partial_value.at[negatives[bucket].reshape(-1)]]
    all_to_all x7 -> x0, waiting for transfers between devices: 34.9 us -> none  [the longest x2 17.7 us: per_device(): lax.all_to_all(input_grad, 'dom', split_axis=1, concat_axis=0, tiled=True)]
    all_to_all x1 -> x0, blocking collectives: 31.8 us -> none  [per_device(): lax.all_to_all(grad_box, 'dom', split_axis=0, concat_axis=1, tiled=True)]
    all_gather x2 -> x0, blocking collectives: 29.9 us -> none  [per_device(): lax.all_gather(right_cur.astype(jnp.bfloat16), 'sub', axis=0, tiled=True)]
  transfers between devices with their start and end apart: 12 -> 0, of which waited for: 6 -> 0; matrix products, arithmetic and copies ran while one was open for 19% -> 0% of each run, Pallas kernels for 0% -> 0%
where the time goes in v1:
time: 190 us
  Pallas kernels  181 us (95%)
  local copies, waits for them, and re-layouts  7.66 us (4%)
    pallas_call x1, Pallas kernels, per_device(): pl.pallas_call(kernel, out_shape=(jax.ShapeDtypeStruct((ROWS, WIDTH), F32...  181 us
    unnamed x23, local copies, waits for them, and re-layouts  7.66 us

profile of v1, /device:TPU:1, one launch (start us, length us, event | category | flops | bytes accessed | tf_op | source)
XLA Modules:
  0.0 189.6 jit_solution(7676378930038229974)
XLA Ops:
  0.6 0.0 copy-start.8
  0.6 0.0 copy-start.6
  0.7 0.8 copy.13.live_ref
  1.4 0.0 copy-done.8
  1.4 0.0 copy-start.4
  1.4 0.0 copy-start.5
  1.4 0.0 copy-start.7
  1.4 0.0 copy-done.6
  1.4 0.7 copy-done.4
  2.1 0.0 copy-done.5
  2.1 0.0 copy-done.7
  2.1 0.0 copy-start
  2.1 1.0 copy-done
  3.2 0.0 copy-start.1
  3.2 1.0 copy-done.1
  4.2 0.0 copy-start.2
  4.2 0.9 copy-done.2
  5.2 0.0 copy-start.3
  5.2 0.7 copy-done.3
  5.9 181.3 %shard_map.121 = (f32[512,256]{1,0:T(8,128)S(1)}, f32[256,256]{1,0:T(8,128)S(1)}, f32[4,256,256]{2,1,0:T(8,128)S(1)}) custom-call(f32[512,256]{1,0:T(8,128)S(1)} %copy-done, f32[1,512]{1,0:T(1,128)S(1)} %bitcast.6, f32[256,256]{1,0:T(8,128)S(1)} %copy-done.2, f32[1,256]{1,0:T(1,128)S(1)} %bitcast.7, bf16[4,256,256]{2,1,0:T(8,128)(2,1)S(1)} %copy-done.1, ...), custom_call_target="tpu_custom_call" | custom-call | tf_op jit(solution)/shard_map/pallas_call | solution.py:357
  187.1 0.8 copy.20
  187.9 0.7 copy.21
  188.6 1.0 copy.22
  (1 shorter events, 0.0 us)
Async XLA Ops:
  0.6 0.8 copy-start.8
  0.6 0.8 copy-start.6
  1.4 0.7 copy-start.4
  1.4 0.7 copy-start.5
  1.4 0.7 copy-start.7
  2.1 1.0 copy-start
  3.2 1.0 copy-start.1
  4.2 0.9 copy-start.2
  5.2 0.7 copy-start.3

commit v2 on v1

v2 whole, which is shorter than its diff:
```python
import jax
import jax.numpy as jnp
from jax import lax
from jax.experimental import pallas as pl
from jax.experimental.pallas import tpu as pltpu
from jax.sharding import PartitionSpec as P

LEARNING_RATE = 0.1
STABILIZER = 1e-06
MESH = pl.DeviceIdType.MESH
F32 = jnp.float32
BF16 = jnp.bfloat16
NX, NY, NZ = 4, 4, 8
DOM = NX * NY * NZ
WIDTH = 256
EDGES = 512
SLOTS = 1024
ROWS = 512
BLOCK = 1024
PART = 256
NEG = 1024


def dot(a, b):
    return lax.dot_general(a, b, (((1,), (0,)), ((), ())), preferred_element_type=F32)


def dot_bt(a, b):
    return lax.dot_general(a, b, (((1,), (1,)), ((), ())), preferred_element_type=F32)


def dot_at(a, b):
    return lax.dot_general(a, b, (((0,), (0,)), ((), ())), preferred_element_type=F32)


def iota(shape, dim):
    return lax.broadcasted_iota(jnp.int32, shape, dim)


def onehot(hit):
    return jnp.where(hit, 1.0, 0.0).astype(BF16)


def pack(rows):
    n = rows.shape[0] // 8
    low = rows[:, :128].reshape(n, 8, 128)
    high = rows[:, 128:].reshape(n, 8, 128)
    return jnp.concatenate([low, high], axis=1).astype(BF16)


def unpack(chunks):
    n = chunks.shape[0]
    wide = chunks.astype(F32)
    low = wide[:, :8].reshape(n * 8, 128)
    high = wide[:, 8:].reshape(n * 8, 128)
    return jnp.concatenate([low, high], axis=1)


def place():
    me = lax.axis_index("dom")
    sub = lax.axis_index("sub")
    return me // (NY * NZ), (me // NZ) % NY, me % NZ, sub // 2, sub % 2


ALONG_Z = ((0, 0), (0, 1), (1, 0), (1, 1), (7, 0), (7, 1), (2, 0), (6, 0))
BACKWARD = (0, 1, 4, 5, 2, 3, 7, 6)


def each_partner(sign, dx, visit):
    mx, my, mz, yh, core = place()
    mine = (mx * NY + my) * NZ
    qx = lax.rem(mx + (dx if sign > 0 else NX - dx), NX)
    for dy in range(NY):
        qy = lax.rem(my + dy, NY)
        if dy == 0:
            flips = (0, 0)
        elif dy == 1:
            flips = (jnp.where(my == NY - 1, 1, 0),) * 2
        elif dy == NY - 1:
            flips = (jnp.where(my == 0, 1, 0),) * 2
        else:
            flips = (core, lax.rem(mx + qx, 2))
        base = (qx * NY + qy) * NZ
        for j, (dz, other_core) in enumerate(ALONG_Z):
            z = lax.rem(mz + dz, NZ)
            there = 1 - core if other_core else core
            sub = lax.rem(yh + flips[other_core], 2) * 2 + there
            owner = base + lax.rem(z + 4 * there, NZ)
            visit(owner, base + j, mine + BACKWARD[j], (base + z, sub), dy == 0 and j == 0)


def kernel(
    left_hbm, lstate_hbm, right_hbm, rstate_hbm, rel_hbm, lids_hbm, rids_hbm, rels_hbm, negs_hbm, live_hbm,
    left_out, right_out, rel_out,
    left_now, lstate_ref, right_now, rstate_ref, rel_now, lids_ref, rids_ref, rels_ref, negs_ref, live_ref,
    send, recv, to_slot, from_slot, row_slot, slot_row, ids, counts, rel_t, inbox, total, moved, edge_grad, weights,
    blk, part, part_in, half, half_in, lstate, rstate, shift_e, shift_e_in, shift_s, shift_s_in, rel_acc, rel_send, rel_in, rel_sum,
    a2a_s, a2a_r, gat_s, gat_r, red_s, red_r, shf_s, shf_r, rel_s, rel_r, sum_s, sum_r, swp_s, swp_r, load_s,
):
    me = lax.axis_index("dom")
    sub = lax.axis_index("sub")
    mx, my, mz, yh, core = place()
    across_z = (mx * NY + my) * NZ + lax.rem(mz + 4, NZ)
    home = jnp.where(core == 0, me, across_z)
    following = (lax.rem(me + 1, DOM), sub)
    previous = (lax.rem(me + DOM - 1, DOM), sub)
    relatives = [(me, lax.rem(sub // 2 + o // 2, 2) * 2 + lax.rem(core + o % 2, 2)) for o in (1, 2, 3)]

    sources = (left_hbm, lstate_hbm, right_hbm, rstate_hbm, rel_hbm, lids_hbm, rids_hbm, rels_hbm, negs_hbm, live_hbm)
    places = (left_now, lstate_ref, right_now, rstate_ref, rel_now, lids_ref, rids_ref, rels_ref, negs_ref, live_ref)
    copies = [pltpu.make_async_copy(src, dst, load_s.at[i]) for i, (src, dst) in enumerate(zip(sources, places))]
    for i in (7, 5, 6, 1, 3, 9, 0, 2, 8):
        copies[i].start()
    barrier = pltpu.get_barrier_semaphore()

    def greet(device):
        pl.semaphore_signal(barrier, inc=1, device_id=device, device_id_type=MESH)

    def planes(body):
        def step(dx, carry):
            body(dx)
            return carry

        lax.fori_loop(0, NX, step, 0)

    def greet_plane(dx):
        def visit(owner, other, there, device, first):
            if first:
                pl.when(dx != 0)(lambda: greet(device))
            else:
                greet(device)

        each_partner(1, dx, visit)

    planes(greet_plane)
    for device in relatives + [following, previous] + [(across_z, o) for o in range(4)]:
        greet(device)

    def remote(src, dst, send_sem, recv_sem, device):
        return pltpu.make_async_remote_copy(
            src_ref=src, dst_ref=dst, send_sem=send_sem, recv_sem=recv_sem, device_id=device, device_id_type=MESH
        )

    def blocks(count, body):
        def step(i, carry):
            body(i)
            return carry

        lax.fori_loop(0, count, step, 0)

    def plane_at(sign, dx):
        return lax.rem(mx + (dx if sign > 0 else NX - dx), NX)

    def send_plane(k, dx):
        outward = k % 2 == 0

        def visit(owner, other, there, device, first):
            chunk, landing = (owner, there) if outward else (other, home)
            copy = remote(send.at[k % 2, chunk], recv.at[k, landing], a2a_s.at[k], a2a_r.at[k, dx], device)
            if first:
                pl.when(dx != 0)(copy.start)

                @pl.when(dx == 0)
                def _():
                    pltpu.make_async_copy(send.at[k % 2, chunk], recv.at[k, landing], a2a_r.at[k, dx]).start()
            else:
                copy.start()

        each_partner(1 if outward else -1, dx, visit)

    def sent(k):
        most = send.at[k % 2, pl.ds(0, DOM - 1)]
        pltpu.make_async_copy(most, most, a2a_s.at[k]).wait()

    def arrived(k, dx):
        plane = recv.at[k, pl.ds(0, 32)]
        pltpu.make_async_copy(plane, plane, a2a_r.at[k, dx]).wait()
        return plane_at(-1 if k % 2 == 0 else 1, dx)

    for i in (1, 3, 5, 6, 7, 9):
        copies[i].wait()
    loads = [copies[i] for i in (0, 2, 8)]
    rows = jnp.concatenate(
        [rels_ref[0].astype(F32), rels_ref[1].astype(F32), lids_ref[...].astype(F32), rids_ref[...].astype(F32), lstate_ref[...],
         jnp.zeros((1, EDGES), F32)], axis=0)
    ids[...] = jnp.transpose(rows)
    lstate[...] = ids[:, 6:7]
    rstate[...] = jnp.transpose(jnp.broadcast_to(rstate_ref[...], (8, PART)))[:, 0:1]

    def index_work(r, stage):
        if stage == 0:
            rel_row = rels_ref[r].astype(F32)
            rel_col = ids[:, r : r + 1]
            same = rel_row == rel_col
            lane, line = iota((EDGES, EDGES), 1), iota((EDGES, EDGES), 0)
            row_rank = jnp.sum(jnp.where(same & (line < lane), 1.0, 0.0), axis=0, keepdims=True)
            col_rank = jnp.sum(jnp.where(same & (lane < line), 1.0, 0.0), axis=1, keepdims=True)
            ids[:, 7:8] = 2.0 * rel_col + col_rank
            row_ids = (2.0 * rel_row + row_rank).astype(jnp.int32)
            gather = onehot(iota((EDGES, ROWS), 1) == ids[:, 2 + r : 3 + r].astype(jnp.int32))

            def fill(i):
                place_of = onehot(iota((256, EDGES), 0) + i * 256 == row_ids)
                to_slot[r, i] = place_of
                slot_row[r, i] = dot(place_of, gather).astype(BF16)

            blocks(4, fill)
        else:
            slot = ids[:, 7:8].astype(jnp.int32)
            for i in range(4):
                from_slot[r, i] = onehot(iota((EDGES, 256), 1) + i * 256 == slot)
            scatter = onehot(iota((ROWS, EDGES), 0) == lids_ref[r : r + 1, :])
            for i in range(4):
                row_slot[r, i] = dot(scatter, from_slot[r, i]).astype(BF16)
            for c in range(2):
                named = negs_ref[r, c : c + 1, :]
                high = onehot(iota((16, NEG), 0) == named // 128)
                low = onehot(iota((128, NEG), 0) == named % 128)
                tally = dot_bt(high, low)
                counts[2 * r + c : 2 * r + c + 1, :] = (
                    jnp.concatenate([tally[i : i + 1, :] for i in range(8)], axis=1) * (1.0 / NEG))

    def send_rows(k, table, values):
        def step(dx):
            p = plane_at(1, dx)
            send[k % 2, pl.ds(p * 32, 32)] = pack(dot(table[p], values))
            send_plane(k, dx)

        planes(step)

    def keep(o):
        return (iota((256, WIDTH), 0) % 8) // 2 == o

    def adagrad(value, state, gradient):
        state = state + jnp.mean(gradient * gradient, axis=1, keepdims=True)
        return value - LEARNING_RATE / (jnp.sqrt(state) + STABILIZER) * gradient, state

    def block_copies(r):
        theirs = relatives[1][1]
        return [
            remote(blk.at[r, sub], blk.at[r, sub], gat_s.at[r, 0], gat_r.at[r, 0], relatives[0]),
            remote(blk.at[r, sub], blk.at[r, sub], gat_s.at[r, 1], gat_r.at[r, 1], relatives[1]),
            remote(blk.at[r, theirs], blk.at[r, theirs], gat_s.at[r, 2], gat_r.at[r, 2], relatives[0]),
        ]

    def gather_block(r):
        copies = block_copies(r)
        copies[1].start()
        copies[0].start()

    def pass_block_on(r):
        copies = block_copies(r)
        copies[1].wait_recv()
        copies[2].start()

    def block_ready(r):
        copies = block_copies(r)
        copies[0].wait()
        copies[1].wait_send()
        copies[2].wait()

    def sum_copies(r):
        return [
            remote(part.at[r, 1 - core], part_in.at[r], red_s.at[r, 0], red_r.at[r, 0], relatives[0]),
            remote(half.at[r], half_in.at[r], red_s.at[r, 1], red_r.at[r, 1], relatives[1]),
        ]

    def sum_across(r):
        copies = sum_copies(r)
        copies[0].wait()
        half[r] = (part[r, core, 1 - yh].astype(F32) + part_in[r, 1 - yh].astype(F32)).astype(BF16)
        copies[1].start()

    def right_update(r, value):
        sum_copies(r)[1].wait()
        gradient = part[r, core, yh].astype(F32) + part_in[r, yh].astype(F32) + half_in[r].astype(F32)
        return adagrad(value.astype(F32), rstate[...], gradient)

    index_work(0, 0)
    for copy in loads:
        copy.wait()
    left_bf = left_now[...].astype(BF16)
    blk[0, sub] = right_now[...].astype(BF16)
    pl.semaphore_wait(barrier, DOM - 1 + 9)
    swap = remote(rel_hbm, rel_now, swp_s, swp_r, (across_z, sub))
    pl.when(core == 1)(swap.start)
    pl.when(core == 0)(copies[4].start)
    rel_acc[...] = jnp.zeros((4, WIDTH, WIDTH), F32)

    for r in range(2):
        k = 4 * r
        send_rows(k, slot_row.at[r], left_bf)
        total[...] = jnp.zeros((EDGES, WIDTH), F32)
        if r == 0:
            gather_block(0)
            index_work(0, 1)
            pl.when(core == 1)(swap.wait)
            pl.when(core == 0)(copies[4].wait)
        else:
            value, state = right_update(0, right_now[...])
            shift_e[...] = value.astype(BF16)
            shift_s[...] = jnp.transpose(jnp.broadcast_to(state, (PART, 128)))[0:8, :]
            shifts = [
                remote(shift_e, shift_e_in, shf_s.at[0], shf_r.at[0], following),
                remote(shift_s, shift_s_in, shf_s.at[1], shf_r.at[1], following),
            ]
            for copy in shifts:
                copy.start()
            sent(k - 1)

        def forward(dx):
            p = arrived(k, dx)
            row = unpack(recv[k, pl.ds(p * 32, 32)])
            inbox[r, p] = row.astype(BF16)
            mapped = sum(dot(jnp.where(keep(o), row, 0.0).astype(BF16), rel_now[o]) for o in range(4))
            send[(k + 1) % 2, pl.ds(p * 32, 32)] = pack(mapped)
            send_plane(k + 1, dx)

        planes(forward)
        if r == 0:
            for o in range(4):
                rel_t[o] = jnp.transpose(rel_now[o].astype(F32)).astype(BF16)
            index_work(1, 0)
            index_work(1, 1)
        else:
            for copy in shifts:
                copy.wait_recv()
            blk[1, sub] = shift_e_in[...]
            gather_block(1)
            rstate[...] = jnp.transpose(shift_s_in[...])[:, 0:1]
        if r == 0:
            pass_block_on(r)

        def settle(dx):
            if r == 1:
                pl.when(dx == NX - 1)(lambda: pass_block_on(1))
            p = arrived(k + 1, dx)
            total[...] += dot(from_slot[r, p], unpack(recv[k + 1, pl.ds(p * 32, 32)]).astype(BF16))

        planes(settle)
        moved[...] = total[...].astype(BF16)
        total[...] = jnp.zeros((EDGES, WIDTH), F32)
        block_ready(r)

        live = live_ref[:, r : r + 1]

        def score(i):
            at = pl.ds(i * 128, 128)
            y = moved[at, :]
            scores = jnp.concatenate([dot_bt(y, blk[r, j]) for j in range(4)], axis=1)
            mask = jnp.where(iota((128, 1), 0) + i * 128 < live, 1.0, 0.0)
            named = iota((128, BLOCK), 1) == ids[at, 4 + r : 5 + r].astype(jnp.int32)
            positive = jnp.sum(jnp.where(named, scores, 0.0), axis=1, keepdims=True)
            pull = -jax.nn.sigmoid(-positive) * mask
            push = jax.nn.sigmoid(scores) * counts[pl.ds(2 * r + i // 2, 1), :] * mask
            weight = (push + jnp.where(named, pull, 0.0)).astype(BF16)
            weights[at, :] = weight
            grad = sum(dot(weight[:, j * 256 : (j + 1) * 256], blk[r, j]) for j in range(4))
            edge_grad[at, :] = grad.astype(BF16)

        blocks(4, score)
        sent(k)
        send_rows(k + 2, to_slot.at[r], edge_grad[...])
        for j in range(4):
            part[r, j % 2, j // 2] = dot_at(weights[:, j * 256 : (j + 1) * 256], moved[...]).astype(BF16)
        sum_copies(r)[0].start()
        sent(k + 1)

        def backward(dx):
            pl.when(dx == 1)(lambda: sum_across(r))
            p = arrived(k + 2, dx)
            row = unpack(recv[k + 2, pl.ds(p * 32, 32)])
            kept = [jnp.where(keep(o), row, 0.0).astype(BF16) for o in range(4)]
            send[(k + 3) % 2, pl.ds(p * 32, 32)] = pack(sum(dot(kept[o], rel_t[o]) for o in range(4)))
            send_plane(k + 3, dx)
            for o in range(4):
                rel_acc[o] += dot_at(inbox[r, p], kept[o])

        planes(backward)
        if r == 1:
            for o in range(4):
                rel_send[o] = rel_acc[o].astype(BF16)
                stays = (core == 0) & (sub == o)
                pl.when(stays)(pltpu.make_async_copy(rel_send.at[o], rel_in.at[sub], rel_r.at[sub]).start)
                pl.when(jnp.logical_not(stays))(
                    remote(rel_send.at[o], rel_in.at[sub], rel_s.at[o], rel_r.at[sub], (home, o)).start)

        def settle_back(dx):
            p = arrived(k + 3, dx)
            total[...] += dot(row_slot[r, p], unpack(recv[k + 3, pl.ds(p * 32, 32)]).astype(BF16))

        planes(settle_back)
        sent(k + 2)
        value, state = adagrad(left_now[...], lstate[...], total[...])
        if r == 0:
            left_now[...] = value
            lstate[...] = state
            left_bf = value.astype(BF16)
        else:
            left_out[...] = value
            value, state = right_update(1, shift_e_in[...])
            right_out[...] = value
    for o in range(4):
        pltpu.make_async_copy(rel_in.at[o], rel_in.at[o], rel_r.at[o]).wait()
    rel_sum[sub] = sum(rel_in[o].astype(F32) for o in range(4)).astype(BF16)
    shares = [
        remote(rel_sum.at[sub], rel_sum.at[sub], sum_s.at[0], sum_r.at[0], relatives[0]),
        remote(rel_sum.at[sub], rel_sum.at[sub], sum_s.at[1], sum_r.at[1], relatives[1]),
        remote(rel_sum.at[relatives[1][1]], rel_sum.at[relatives[1][1]], sum_s.at[2], sum_r.at[2], relatives[0]),
    ]
    shares[1].start()
    shares[0].start()
    rel_out[sub] = rel_sum[sub].astype(F32)
    shares[1].wait_recv()
    shares[2].start()
    rel_out[relatives[1][1]] = rel_sum[relatives[1][1]].astype(F32)
    shares[0].wait_recv()
    rel_out[relatives[0][1]] = rel_sum[relatives[0][1]].astype(F32)
    shares[2].wait_recv()
    rel_out[relatives[2][1]] = rel_sum[relatives[2][1]].astype(F32)
    for copy in shares:
        copy.wait_send()
    for o in range(4):
        stays = (core == 0) & (sub == o)
        pl.when(jnp.logical_not(stays))(
            remote(rel_send.at[o], rel_in.at[sub], rel_s.at[o], rel_r.at[sub], (home, o)).wait_send)
    for copy in shifts:
        copy.wait_send()
    sent(7)


def per_device(left_emb, left_state, right_emb, right_state, rel_ops, left_ids, right_ids, relations, negatives, live):
    vmem = pltpu.VMEM
    dma = pltpu.SemaphoreType.DMA
    whole = pl.BlockSpec(memory_space=pltpu.VMEM)
    return pl.pallas_call(
        kernel,
        out_shape=(
            jax.ShapeDtypeStruct((ROWS, WIDTH), F32),
            jax.ShapeDtypeStruct((PART, WIDTH), F32),
            jax.ShapeDtypeStruct((4, WIDTH, WIDTH), F32),
        ),
        in_specs=[pl.BlockSpec(memory_space=pl.ANY)] * 10,
        out_specs=[whole] * 3,
        scratch_shapes=[
            vmem((ROWS, WIDTH), F32),
            vmem((1, ROWS), F32),
            vmem((PART, WIDTH), F32),
            vmem((1, PART), F32),
            vmem((4, WIDTH, WIDTH), BF16),
            vmem((2, EDGES), jnp.int32),
            vmem((2, EDGES), jnp.int32),
            vmem((2, 1, EDGES), jnp.int32),
            vmem((2, 2, NEG), jnp.int32),
            vmem((1, 2), jnp.int32),
            vmem((2, DOM, 16, 128), BF16),
            vmem((8, DOM, 16, 128), BF16),
            vmem((2, 4, 256, EDGES), BF16),
            vmem((2, 4, EDGES, 256), BF16),
            vmem((2, 4, ROWS, 256), BF16),
            vmem((2, 4, 256, ROWS), BF16),
            vmem((EDGES, 8), F32),
            vmem((8, BLOCK), F32),
            vmem((4, WIDTH, WIDTH), BF16),
            vmem((2, 4, 256, WIDTH), BF16),
            vmem((EDGES, WIDTH), F32),
            vmem((EDGES, WIDTH), BF16),
            vmem((EDGES, WIDTH), BF16),
            vmem((EDGES, BLOCK), BF16),
            vmem((2, 4, PART, WIDTH), BF16),
            vmem((2, 2, 2, PART, WIDTH), BF16),
            vmem((2, 2, PART, WIDTH), BF16),
            vmem((2, PART, WIDTH), BF16),
            vmem((2, PART, WIDTH), BF16),
            vmem((ROWS, 1), F32),
            vmem((PART, 1), F32),
            vmem((PART, WIDTH), BF16),
            vmem((PART, WIDTH), BF16),
            vmem((8, PART), F32),
            vmem((8, PART), F32),
            vmem((4, WIDTH, WIDTH), F32),
            vmem((4, WIDTH, WIDTH), BF16),
            vmem((4, WIDTH, WIDTH), BF16),
            vmem((4, WIDTH, WIDTH), BF16),
            dma((8,)), dma((8, 4)), dma((2, 3)), dma((2, 3)), dma((2, 2)), dma((2, 2)),
            dma((2,)), dma((2,)), dma((4,)), dma((4,)), dma((3,)), dma((3,)), dma, dma, dma((10,)),
        ],
        compiler_params=pltpu.CompilerParams(collective_id=0, has_side_effects=True, vmem_limit_bytes=56 << 20),
    )(
        left_emb, left_state.reshape(1, -1), right_emb, right_state.reshape(1, -1), rel_ops, left_ids, right_ids,
        jnp.swapaxes(relations, 1, 2), negatives, live.T,
    )


def solution(mesh):
    placed = (
        P(("dom", "sub"), None),
        P(("dom", "sub")),
        P(("dom", "sub"), None),
        P(("dom", "sub")),
        P("dom", None, None),
        P(None, ("dom", "sub")),
        P(None, ("dom", "sub")),
        P(None, ("dom", "sub"), None),
        P(None, ("dom", "sub"), None),
        P(None, ("dom", "sub")),
    )
    return jax.shard_map(
        per_device,
        mesh=mesh,
        in_specs=placed,
        out_specs=(P(("dom", "sub"), None), P(("dom", "sub"), None), P("dom", None, None)),
        check_vma=False,
    )
```

time: 190 us -> 152 us (0.80)
  the two profiles are of different devices: /device:TPU:1 before, /device:TPU:59 now
where the time goes in v2:
time: 152 us
  Pallas kernels  146 us (96%)
  local copies, waits for them, and re-layouts  4.6 us (3%)
    pallas_call x1, Pallas kernels, per_device(): pl.pallas_call(kernel, out_shape=(jax.ShapeDtypeStruct((ROWS, WIDTH), F32...  146 us
    unnamed x5, local copies, waits for them, and re-layouts  4.6 us

profile of v2, /device:TPU:59, one launch (start us, length us, event | category | flops | bytes accessed | tf_op | source)
XLA Modules:
  0.0 151.6 jit_solution(6351175748394383106)
XLA Ops:
  0.6 146.3 %shard_map.121 = (f32[512,256]{1,0:T(8,128)}, f32[256,256]{1,0:T(8,128)}, f32[4,256,256]{2,1,0:T(8,128)}) custom-call(f32[512,256]{1,0:T(8,128)} %left_hbm.1, f32[1,512]{1,0:T(1,128)} %bitcast.5, f32[256,256]{1,0:T(8,128)} %right_hbm.1, f32[1,256]{1,0:T(1,128)} %bitcast.6, bf16[4,256,256]{2,1,0:T(8,128)(2,1)} %rel_hbm.1, s32[2,512]{1,0:T(2,128)} %lids_hbm.1, ...), custom_call_target="tpu_custom_call" | custom-call | tf_op jit(solution)/shard_map/pallas_call | solution.py:436
  147.0 0.0 copy-start
  147.0 2.0 %copy.16 = f32[512,256]{1,0:T(8,128)} copy(f32[512,256]{1,0:T(8,128)} %get-tuple-element.6) | data formatting | bytes 1048576
  149.0 1.7 %copy.17 = f32[256,256]{1,0:T(8,128)} copy(f32[256,256]{1,0:T(8,128)} %get-tuple-element.7) | data formatting | bytes 524288
  150.6 0.0 copy-done
  150.6 1.0 copy.18
Async XLA Ops:
  147.0 3.6 %copy-start = (f32[4,256,256]{2,1,0:T(8,128)S(1)}, f32[4,256,256]{2,1,0:T(8,128)}, u32[]{:S(2)}) copy-start(f32[4,256,256]{2,1,0:T(8,128)} %get-tuple-element.8) | copy-start | bytes 3145732

commit v3 on v2

--- a/solution.py
+++ b/solution.py
@@ -123,6 +123,10 @@
 
         lax.fori_loop(0, NX, step, 0)
 
+    def unrolled(body):
+        for dx in range(NX):
+            body(dx)
+
     def greet_plane(dx):
         def visit(owner, other, there, device, first):
             if first:
@@ -158,11 +162,10 @@
             chunk, landing = (owner, there) if outward else (other, home)
             copy = remote(send.at[k % 2, chunk], recv.at[k, landing], a2a_s.at[k], a2a_r.at[k, dx], device)
             if first:
-                pl.when(dx != 0)(copy.start)
-
-                @pl.when(dx == 0)
-                def _():
+                if dx == 0:
                     pltpu.make_async_copy(send.at[k % 2, chunk], recv.at[k, landing], a2a_r.at[k, dx]).start()
+                else:
+                    copy.start()
             else:
                 copy.start()
 
@@ -226,7 +229,7 @@
             send[k % 2, pl.ds(p * 32, 32)] = pack(dot(table[p], values))
             send_plane(k, dx)
 
-        planes(step)
+        unrolled(step)
 
     def keep(o):
         return (iota((256, WIDTH), 0) % 8) // 2 == o
@@ -316,7 +319,7 @@
             send[(k + 1) % 2, pl.ds(p * 32, 32)] = pack(mapped)
             send_plane(k + 1, dx)
 
-        planes(forward)
+        unrolled(forward)
         if r == 0:
             for o in range(4):
                 rel_t[o] = jnp.transpose(rel_now[o].astype(F32)).astype(BF16)
@@ -367,7 +370,8 @@
         sent(k + 1)
 
         def backward(dx):
-            pl.when(dx == 1)(lambda: sum_across(r))
+            if dx == 1:
+                sum_across(r)
             p = arrived(k + 2, dx)
             row = unpack(recv[k + 2, pl.ds(p * 32, 32)])
             kept = [jnp.where(keep(o), row, 0.0).astype(BF16) for o in range(4)]
@@ -376,7 +380,7 @@
             for o in range(4):
                 rel_acc[o] += dot_at(inbox[r, p], kept[o])
 
-        planes(backward)
+        unrolled(backward)
         if r == 1:
             for o in range(4):
                 rel_send[o] = rel_acc[o].astype(BF16)
@@ -410,14 +414,14 @@
     ]
     shares[1].start()
     shares[0].start()
-    rel_out[sub] = rel_sum[sub].astype(F32)
+    rel_out[sub] = rel_sum[sub]
     shares[1].wait_recv()
     shares[2].start()
-    rel_out[relatives[1][1]] = rel_sum[relatives[1][1]].astype(F32)
+    rel_out[relatives[1][1]] = rel_sum[relatives[1][1]]
     shares[0].wait_recv()
-    rel_out[relatives[0][1]] = rel_sum[relatives[0][1]].astype(F32)
+    rel_out[relatives[0][1]] = rel_sum[relatives[0][1]]
     shares[2].wait_recv()
-    rel_out[relatives[2][1]] = rel_sum[relatives[2][1]].astype(F32)
+    rel_out[relatives[2][1]] = rel_sum[relatives[2][1]]
     for copy in shares:
         copy.wait_send()
     for o in range(4):
@@ -429,17 +433,26 @@
     sent(7)
 
 
+def place_results(left, right, rel, left_out, right_out, rel_out):
+    left_out[...] = left[...]
+    right_out[...] = right[...]
+    rel_out[...] = rel[...].astype(F32)
+
+
 def per_device(left_emb, left_state, right_emb, right_state, rel_ops, left_ids, right_ids, relations, negatives, live):
     vmem = pltpu.VMEM
     dma = pltpu.SemaphoreType.DMA
     whole = pl.BlockSpec(memory_space=pltpu.VMEM)
-    return pl.pallas_call(
-        kernel,
-        out_shape=(
+    def shapes(rel_type):
+        return (
             jax.ShapeDtypeStruct((ROWS, WIDTH), F32),
             jax.ShapeDtypeStruct((PART, WIDTH), F32),
-            jax.ShapeDtypeStruct((4, WIDTH, WIDTH), F32),
-        ),
+            jax.ShapeDtypeStruct((4, WIDTH, WIDTH), rel_type),
+        )
+
+    results = pl.pallas_call(
+        kernel,
+        out_shape=shapes(BF16),
         in_specs=[pl.BlockSpec(memory_space=pl.ANY)] * 10,
         out_specs=[whole] * 3,
         scratch_shapes=[
@@ -490,6 +503,12 @@
         left_emb, left_state.reshape(1, -1), right_emb, right_state.reshape(1, -1), rel_ops, left_ids, right_ids,
         jnp.swapaxes(relations, 1, 2), negatives, live.T,
     )
+    return pl.pallas_call(
+        place_results,
+        out_shape=shapes(F32),
+        in_specs=[whole] * 3,
+        out_specs=[whole] * 3,
+    )(*results)
 
 
 def solution(mesh):

time: 152 us -> 151 us (level)
  the two profiles are of different devices: /device:TPU:59 before, /device:TPU:1 now
where the time goes in v3:
time: 151 us
  Pallas kernels  150 us (99%)
    pallas_call x1, Pallas kernels, per_device(): pl.pallas_call(kernel, out_shape=shapes(BF16), in_specs=[pl.BlockSpec(mem...  148 us

profile of v3, /device:TPU:1, one launch (start us, length us, event | category | flops | bytes accessed | tf_op | source)
XLA Modules:
  0.0 150.8 jit_solution(11984826810503076730)
XLA Ops:
  0.6 147.6 %shard_map.121 = (f32[512,256]{1,0:T(8,128)}, f32[256,256]{1,0:T(8,128)}, bf16[4,256,256]{2,1,0:T(8,128)(2,1)}) custom-call(f32[512,256]{1,0:T(8,128)} %left_hbm.1, f32[1,512]{1,0:T(1,128)} %bitcast.5, f32[256,256]{1,0:T(8,128)} %right_hbm.1, f32[1,256]{1,0:T(1,128)} %bitcast.6, bf16[4,256,256]{2,1,0:T(8,128)(2,1)} %rel_hbm.1, s32[2,512]{1,0:T(2,128)} %lids_hbm.1, ...), custom_call_target="tpu_custom_call" | custom-call | tf_op jit(solution)/shard_map/pallas_call | solution.py:453
  148.2 2.5 %shard_map.122 = (f32[512,256]{1,0:T(8,128)}, f32[256,256]{1,0:T(8,128)}, f32[4,256,256]{2,1,0:T(8,128)}) custom-call(f32[512,256]{1,0:T(8,128)} %get-tuple-element.6.left, f32[256,256]{1,0:T(8,128)} %get-tuple-element.7.right, bf16[4,256,256]{2,1,0:T(8,128)(2,1)} %get-tuple-element.8.rel), custom_call_target="tpu_custom_call" | custom-call | tf_op jit(solution)/shard_map/pallas_call | solution.py:506
